TPU v7x, 32 devices: a whole 2x2x4 slice. The times are simulated.
32 devices in a mesh: sec: 4 (over x, core), tile: 8 (over z, y).
Axes of the slice: x: 2, y: 2, z: 4, core: 2. Of those that a mesh axis runs over, the one named last changes fastest.
Arguments:
- intersection_faces: bfloat16 [256, 1, 128, 128], P(('sec', 'tile')), may hold values from -6 to 6
- destination: int32 [256, 1], P(('sec', 'tile')), may hold values from 0 to 7; in each aligned block of 8 rows (0 to 7, 8 to 15, ...) at most 2 rows name the same one
- partner: int32 [256], P(('sec', 'tile')), may hold values from 0 to 7
- face_peaks: int32 [256, 2, 8], P(('sec', 'tile')), may hold values from 0 to 127
- coarse: bfloat16 [64, 256, 256], P(('sec', 'tile')), may hold values from -6 to 6
- coarse_peaks: int32 [256, 2, 8], P(('sec', 'tile')), may hold values from 0 to 255
- upper_faces: bfloat16 [64, 1, 128, 128], P(('sec', 'tile')), may hold values from -6 to 6
- lower_faces: bfloat16 [64, 1, 128, 128], P(('sec', 'tile')), may hold values from -6 to 6
- section_peaks: int32 [64, 2, 8], P(('sec', 'tile')), may hold values from 0 to 127
Outputs:
- fine_scores: float32 [256, 1, 8], P(('sec', 'tile'))
- coarse_scores: float32 [256, 8], P(('sec', 'tile'))
- section_scores: float32 [64, 1, 8], P(('sec', 'tile'))
Inputs may be any that keep to these rules, and one draw needn't show every extreme that they name: `destination`: in each aligned block of 8 rows (the faces of one device) no value appears more than 2 times.
All inputs are finite; a program needn't handle non-finite values.
Results may differ from a plain program's by a relative error of at most 0.012.
The roundings to bfloat16 on the way count: a program that leaves them out, or rounds other values in their place, can miss the bound.
Values may be sent and summed in bfloat16 or wider, within the bound.
A program may use at most 64 MiB of HBM per device.

v0:
```python
import jax
import jax.numpy as jnp
from jax import lax
from jax.sharding import PartitionSpec as P

TWO_PI = 6.283185307179586


def from_behind(value, axis, steps):
    count = lax.axis_size(axis)
    first, last = (max(0, -steps), min(count, count - steps))
    return lax.ppermute(value, axis, [(source, source + steps) for source in range(first, last)])


def window_weights(extent):
    positions = jnp.arange(extent, dtype=jnp.float32)
    return 0.5 - 0.5 * jnp.cos((positions + 0.5) * (TWO_PI / extent))


def dft_tables(extent):
    indices = jnp.arange(extent, dtype=jnp.int32)
    angles = (indices[:, None] * indices[None, :] % extent).astype(jnp.float32) * (TWO_PI / extent)
    return (jnp.cos(angles).astype(jnp.bfloat16), jnp.sin(angles).astype(jnp.bfloat16))


def spectrum(images):
    extent = images.shape[-1]
    weights = window_weights(extent)
    shaped = (images.astype(jnp.float32) * weights[:, None] * weights[None, :]).astype(jnp.bfloat16)
    cosine, sine_table = dft_tables(extent)
    segment_tables = jnp.stack([cosine, sine_table])
    segment_one = jnp.einsum(
        "jkx,...xy->...jky", segment_tables, shaped, preferred_element_type=jnp.float32
    ).astype(jnp.bfloat16)
    second_tables = jnp.stack(
        [
            jnp.concatenate([cosine, sine_table], axis=1),
            jnp.concatenate([-sine_table, cosine], axis=1),
        ]
    )
    segment_two = jnp.einsum(
        "...jky,jyl->...kl", segment_one, second_tables, preferred_element_type=jnp.float32
    )
    return (segment_two[..., :extent], -segment_two[..., extent:])


def correlate(own_spec, other_spec, peak_marks):
    own_real, own_imag = own_spec
    other_real, other_imag = other_spec
    cross_real = own_real * other_real + own_imag * other_imag
    cross_imag = own_imag * other_real - own_real * other_imag
    magnitude = jnp.sqrt(cross_real * cross_real + cross_imag * cross_imag)
    floor_value = 0.05 * jnp.mean(magnitude, axis=(-2, -1), keepdims=True) + 1e-06
    divisor = jnp.maximum(magnitude, floor_value)
    unit_real = cross_real / divisor
    unit_imag = cross_imag / divisor
    extent = own_real.shape[-1]
    indices = jnp.arange(extent, dtype=jnp.int32)
    row_angles = (peak_marks[..., 0, :, None] * indices % extent).astype(jnp.float32) * (
        TWO_PI / extent
    )
    col_angles = (peak_marks[..., 1, :, None] * indices % extent).astype(jnp.float32) * (
        TWO_PI / extent
    )
    row_cos = jnp.cos(row_angles)
    row_sin = jnp.sin(row_angles)
    high = lax.Precision.HIGHEST
    first_real = jnp.einsum("...pk,...kl->...pl", row_cos, unit_real, precision=high) - jnp.einsum(
        "...pk,...kl->...pl", row_sin, unit_imag, precision=high
    )
    first_imag = jnp.einsum("...pk,...kl->...pl", row_cos, unit_imag, precision=high) + jnp.einsum(
        "...pk,...kl->...pl", row_sin, unit_real, precision=high
    )
    return (
        jnp.sum(first_real * jnp.cos(col_angles) - first_imag * jnp.sin(col_angles), axis=-1)
        / extent
    )


def body(
    intersection_faces,
    destination,
    partner,
    face_peaks,
    coarse,
    coarse_peaks,
    upper_faces,
    lower_faces,
    section_peaks,
):
    face_dev = intersection_faces.shape[0]
    tile_dev = coarse.shape[0]
    per_tile = face_dev // tile_dev
    windows = intersection_faces.shape[1]
    peak_count = face_peaks.shape[2]
    coarse_side = coarse.shape[-1]
    tile_count = lax.axis_size("tile")
    capacity = max(2, (face_dev + tile_count - 1) // tile_count)
    slot_count = tile_count * capacity
    target = destination[:, 0]
    face_order = jnp.arange(face_dev, dtype=jnp.int32)
    earlier = (target[None, :] == target[:, None]) & (face_order[None, :] < face_order[:, None])
    position = jnp.sum(earlier.astype(jnp.int32), axis=1)
    slot_of = target * capacity + position
    slot_match = slot_of[None, :] == jnp.arange(slot_count, dtype=jnp.int32)[:, None]
    filled = jnp.any(slot_match, axis=1)
    source = jnp.sum(jnp.where(slot_match, face_order[None, :], 0), axis=1)
    requests = jnp.where(filled, partner[source] + 1, 0).reshape(tile_count, capacity)
    own_real, own_imag = spectrum(intersection_faces)
    parcel = jnp.where(
        filled[:, None, None, None],
        intersection_faces[source],
        jnp.zeros_like(intersection_faces[source]),
    )
    parcel = parcel.reshape((tile_count, capacity) + intersection_faces.shape[1:])
    peak_marks = face_peaks[source].reshape((tile_count, capacity) + face_peaks.shape[1:])
    got_faces, got_marks, wanted_ids = (
        lax.all_to_all(parcel, "tile", split_axis=0, concat_axis=0, tiled=True),
        lax.all_to_all(peak_marks, "tile", split_axis=0, concat_axis=0, tiled=True),
        lax.all_to_all(requests, "tile", split_axis=0, concat_axis=0, tiled=True),
    )

    def one_slot(packed):
        face_in, mark_in, wanted = packed
        chosen_slot = jnp.maximum(wanted - 1, 0)
        own_part = (own_real[chosen_slot], own_imag[chosen_slot])
        marks_all = mark_in[None]
        scores = correlate(spectrum(face_in), own_part, marks_all)
        return jnp.where(wanted > 0, scores, jnp.zeros_like(scores))

    slot_scores = lax.map(
        one_slot,
        (
            got_faces.reshape((slot_count,) + intersection_faces.shape[1:]),
            got_marks.reshape((slot_count,) + face_peaks.shape[1:]),
            wanted_ids.reshape(slot_count),
        ),
    )
    returned = lax.all_to_all(
        slot_scores.reshape(tile_count, capacity, windows, peak_count),
        "tile",
        split_axis=0,
        concat_axis=0,
        tiled=True,
    )
    fine_scores = returned.reshape(slot_count, windows, peak_count)[slot_of]
    coarse_real, coarse_imag = spectrum(coarse)
    wanted_tile = target * tile_dev + partner // per_tile
    empty_tiles = jnp.zeros((face_dev, coarse_side, coarse_side), jnp.bfloat16)
    shard_rows = lax.all_gather(coarse, "tile", axis=0, tiled=True)
    row_count = shard_rows.shape[0]
    inside = (wanted_tile >= 0) & (wanted_tile < row_count)
    selected = shard_rows[jnp.clip(wanted_tile, 0, row_count - 1)]
    partner_tiles = jnp.where(inside[:, None, None], selected, empty_tiles)

    def coarse_one(packed):
        tile_slot, other_tile, mark_in = packed
        return correlate(
            (coarse_real[tile_slot], coarse_imag[tile_slot]), spectrum(other_tile), mark_in
        )

    coarse_scores = lax.map(coarse_one, (face_order // per_tile, partner_tiles, coarse_peaks))
    lower_in = from_behind(lower_faces, "sec", 1)
    section_marks = section_peaks[:, None]
    section_scores = correlate(spectrum(upper_faces), spectrum(lower_in), section_marks)
    return (fine_scores, coarse_scores, section_scores)


def solution(mesh):
    return jax.shard_map(
        body,
        mesh=mesh,
        in_specs=(
            P(("sec", "tile"), None, None, None),
            P(("sec", "tile"), None),
            P(("sec", "tile")),
            P(("sec", "tile"), None, None),
            P(("sec", "tile"), None, None),
            P(("sec", "tile"), None, None),
            P(("sec", "tile"), None, None, None),
            P(("sec", "tile"), None, None, None),
            P(("sec", "tile"), None, None),
        ),
        out_specs=(
            P(("sec", "tile"), None, None),
            P(("sec", "tile"), None),
            P(("sec", "tile"), None, None),
        ),
        check_vma=False,
    )
```

profile of v0, /device:TPU:0, one launch (start us, length us, event | category | flops | bytes accessed | tf_op | source)
XLA Modules:
  0.0 286.7 jit_solution(2886775491009147244)
XLA Ops:
  9.7 1.3 gather_fusion
  11.7 7.3 %all-to-all-start = ((s32[8,1,2]{2,1,0:T(1,128)}), s32[8,1,2]{2,1,0:T(1,128)}, u32[]{:S(2)}, u32[]{:S(2)}) async-start(s32[8,1,2]{2,1,0:T(1,128)} %bitcast.34), calls=%async_computation | async-start | bytes 8192 | tf_op jit(solution)/shard_map/all_to_all | solution.py:120
  19.0 2.1 collective-permute-start
  22.5 1.2 compare_and_fusion
  25.5 1.1 sine_convert_fusion.5
  26.6 1.1 sine_convert_fusion.4
  27.7 1.4 fusion.275
  34.7 1.6 broadcast_select_fusion.2
  36.8 1.3 gather_fusion.1
  38.1 5.8 %all-to-all-start.1 = ((s32[8,2,2,8]{3,2,1,0:T(2,128)}), s32[8,2,2,8]{3,2,1,0:T(2,128)S(1)}, u32[]{:S(2)}, u32[]{:S(2)}) async-start(s32[8,2,2,8]{3,2,1,0:T(2,128)} %bitcast.35), calls=%async_computation.1 | async-start | bytes 32768 | tf_op jit(solution)/shard_map/all_to_all | solution.py:119
  44.5 1.3 reduce.15
  45.9 1.4 convolution_bitcast_fusion.4
  47.4 3.3 %all-to-all-done.1 = s32[8,2,2,8]{3,2,1,0:T(2,128)S(1)} async-done(((s32[8,2,2,8]{3,2,1,0:T(2,128)}), s32[8,2,2,8]{3,2,1,0:T(2,128)S(1)}, u32[]{:S(2)}, u32[]{:S(2)}) %all-to-all-start.1) | async-done | bytes 1056 | tf_op jit(solution)/shard_map/all_to_all | solution.py:119
  50.7 3.5 %all-to-all-start.2 = ((bf16[8,2,1,128,128]{3,4,1,2,0:T(8,128)(2,1)}), bf16[8,2,1,128,128]{3,4,1,2,0:T(8,128)(2,1)S(1)}, u32[]{:S(2)}, u32[]{:S(2)}) async-start(bf16[8,2,1,128,128]{3,4,1,2,0:T(8,128)(2,1)} %broadcast_select_fusion.2), calls=%async_computation.2 | async-start | bytes 1048576 | tf_op jit(solution)/shard_map/all_to_all | solution.py:118
  55.7 17.7 %all-to-all-done.2 = bf16[8,2,1,128,128]{3,4,1,2,0:T(8,128)(2,1)S(1)} async-done(((bf16[8,2,1,128,128]{3,4,1,2,0:T(8,128)(2,1)}), bf16[8,2,1,128,128]{3,4,1,2,0:T(8,128)(2,1)S(1)}, u32[]{:S(2)}, u32[]{:S(2)}) %all-to-all-start.2) | async-done | bytes 524320 | tf_op jit(solution)/shard_map/all_to_all | solution.py:118
  73.4 112.0 %while.24 = (s32[]{:T(128)}, f32[16,1,8]{2,1,0:T(1,128)}, s32[16]{0:T(128)S(1)}, s32[16,2,8]{2,1,0:T(2,128)S(1)}, bf16[16,1,128,128]{2,3,1,0:T(8,128)(2,1)S(1)},...) while((s32[]{:T(128)}, f32[16,1,8]{2,1,0:T(1,128)}, ...), condition=%wide.region_6.7_spmd, body=%wide.region_3.6_spmd.sunk | while | flops 33161740 | bytes 1723514 | solution.py:131
  76.9 1.5 fusion.332
  83.9 1.5 fusion.332
  90.9 1.5 fusion.332
  97.8 1.5 fusion.332
  104.8 1.5 fusion.332
  111.8 1.5 fusion.332
  118.8 1.5 fusion.332
  125.8 1.5 fusion.332
  132.8 1.5 fusion.332
  139.8 1.5 fusion.332
  146.7 1.5 fusion.332
  153.8 1.5 fusion.332
  160.8 1.5 fusion.332
  167.8 1.5 fusion.332
  174.8 1.5 fusion.332
  181.8 1.5 fusion.332
  185.4 3.6 %all-to-all-start.3 = ((f32[8,2,1,8]{3,1,2,0:T(2,128)}), f32[8,2,1,8]{3,1,2,0:T(2,128)S(1)}, u32[]{:S(2)}, u32[]{:S(2)}) async-start(f32[8,2,1,8]{3,1,2,0:T(2,128)} %bitcast.56), calls=%async_computation.3 | async-start | bytes 16384 | tf_op jit(solution)/shard_map/all_to_all | solution.py:139
  189.6 5.7 %all-to-all-done.3 = f32[8,2,1,8]{3,1,2,0:T(2,128)S(1)} async-done(((f32[8,2,1,8]{3,1,2,0:T(2,128)}), f32[8,2,1,8]{3,1,2,0:T(2,128)S(1)}, u32[]{:S(2)}, u32[]{:S(2)}) %all-to-all-start.3) | async-done | bytes 544 | tf_op jit(solution)/shard_map/all_to_all | solution.py:139
  195.3 1.3 gather_fusion.3
  196.6 2.3 gather_fusion.4
  199.1 80.1 %while.25 = (s32[]{:T(128)}, f32[8,8]{1,0:T(8,128)S(1)}, s32[8,2,8]{2,1,0:T(2,128)}, s32[8]{0:T(128)S(1)}, f32[2,256,256]{2,1,0:T(8,128)S(1)}, /*index=5*/bf16[8...) while((s32[]{:T(128)}, f32[8,8]{1,0:T(8,128)S(1)}, ...), condition=%wide.region_10.11_spmd, body=%wide.region_7.10_spmd.sunk | while | flops 232903680 | bytes 6737723 | solution.py:162
  203.4 1.1 sine_convert_fusion.15
  204.5 1.1 sine_convert_fusion.14
  213.4 1.1 sine_convert_fusion.15
  214.5 1.1 sine_convert_fusion.14
  223.4 1.1 sine_convert_fusion.15
  224.5 1.1 sine_convert_fusion.14
  233.4 1.1 sine_convert_fusion.15
  234.5 1.1 sine_convert_fusion.14
  253.5 1.1 sine_convert_fusion.15
  254.6 1.1 sine_convert_fusion.14
  273.5 1.1 sine_convert_fusion.15
  (452 shorter events, 118.5 us)
Async XLA Ops:
  7.2 29.6 %copy-start = (s32[8,2,8]{2,1,0:T(2,128)S(1)}, s32[8,2,8]{2,1,0:T(2,128)}, u32[]{:S(2)}) copy-start(s32[8,2,8]{2,1,0:T(2,128)} %param.16) | copy-start | bytes 1540
  7.2 23.1 %copy-start.4 = (bf16[2,256,256]{2,1,0:T(8,128)(2,1)S(1)}, bf16[2,256,256]{2,1,0:T(8,128)(2,1)}, u32[]{:S(2)}) copy-start(bf16[2,256,256]{2,1,0:T(8,128)(2,1)} %param.17) | copy-start | bytes 786436
  7.2 189.4 %all-gather.2.cloned.1.call-start = ((), (), s32[]{:S(2)}) async-start(), calls=%async_computation.4 | async-start | bytes 2359296 | tf_op jit(solution)/shard_map/all_gather | solution.py:150
  9.7 23.2 %copy-start.7 = (s32[1024]{0:T(1024)}, s32[1024]{0:T(1024)S(1)}, u32[]{:S(2)}) copy-start(s32[1024]{0:T(1024)S(1)} %pad_clamp_fusion.2) | copy-start | bytes 12292
  11.7 26.4 %all-to-all-start = ((s32[8,1,2]{2,1,0:T(1,128)}), s32[8,1,2]{2,1,0:T(1,128)}, u32[]{:S(2)}, u32[]{:S(2)}) async-start(s32[8,1,2]{2,1,0:T(1,128)} %bitcast.34), calls=%async_computation | async-start | bytes 8192 | tf_op jit(solution)/shard_map/all_to_all | solution.py:120
  19.0 26.9 %collective-permute-start = (bf16[2,1,128,128]{3,2,1,0:T(8,128)(2,1)}, bf16[2,1,128,128]{3,2,1,0:T(8,128)(2,1)}, u32[]{:S(2)}, u32[]{:S(2)}) collective-permute-start(bf16[2,1,128,128]{3,2,1,0:T(8,128)(2,1)} %param.20), channel_id=1, source_target_pairs={{0,8},{8,16},{16,24},{1,9},{9,17},{17,25},{2,10},{10,18},{18,26},{... | collective-permute-start | bytes 196616 | tf_op jit(solution)/shard_map/ppermute | solution.py:12
  24.2 8.7 %copy-start.2 = (bf16[1,128,128]{2,1,0:T(8,128)(2,1)}, bf16[1,128,128]{2,1,0:T(8,128)(2,1)S(1)}, u32[]{:S(2)}) copy-start(bf16[1,128,128]{2,1,0:T(8,128)(2,1)S(1)} %get-tuple-element.303) | copy-start | bytes 98308
  24.2 8.7 %copy-start.3 = (bf16[1,128,128]{2,1,0:T(8,128)(2,1)}, bf16[1,128,128]{2,1,0:T(8,128)(2,1)S(1)}, u32[]{:S(2)}) copy-start(bf16[1,128,128]{2,1,0:T(8,128)(2,1)S(1)} %get-tuple-element.304) | copy-start | bytes 98308
  30.3 1.0 copy-start.5
  31.2 1.0 copy-start.1
  34.7 20.3 %copy-start.6 = (s32[2,1,1,8]{3,2,0,1:T(1,128)S(1)}, s32[2,1,1,8]{3,2,0,1:T(1,128)}, u32[]{:S(2)}) copy-start(s32[2,1,1,8]{3,2,0,1:T(1,128)} %get-tuple-element.299) | copy-start | bytes 196
  38.1 12.6 %all-to-all-start.1 = ((s32[8,2,2,8]{3,2,1,0:T(2,128)}), s32[8,2,2,8]{3,2,1,0:T(2,128)S(1)}, u32[]{:S(2)}, u32[]{:S(2)}) async-start(s32[8,2,2,8]{3,2,1,0:T(2,128)} %bitcast.35), calls=%async_computation.1 | async-start | bytes 32768 | tf_op jit(solution)/shard_map/all_to_all | solution.py:119
  50.7 22.7 %all-to-all-start.2 = ((bf16[8,2,1,128,128]{3,4,1,2,0:T(8,128)(2,1)}), bf16[8,2,1,128,128]{3,4,1,2,0:T(8,128)(2,1)S(1)}, u32[]{:S(2)}, u32[]{:S(2)}) async-start(bf16[8,2,1,128,128]{3,4,1,2,0:T(8,128)(2,1)} %broadcast_select_fusion.2), calls=%async_computation.2 | async-start | bytes 1048576 | tf_op jit(solution)/shard_map/all_to_all | solution.py:118
  185.4 13.5 %copy-start.8 = (pred[8]{0:T(512)(128)(4,1)S(1)}, pred[8]{0:T(512)(128)(4,1)}, u32[]{:S(2)}) copy-start(pred[8]{0:T(512)(128)(4,1)} %get-tuple-element.265) | copy-start | bytes 28
  185.4 9.9 %all-to-all-start.3 = ((f32[8,2,1,8]{3,1,2,0:T(2,128)}), f32[8,2,1,8]{3,1,2,0:T(2,128)S(1)}, u32[]{:S(2)}, u32[]{:S(2)}) async-start(f32[8,2,1,8]{3,1,2,0:T(2,128)} %bitcast.56), calls=%async_computation.3 | async-start | bytes 16384 | tf_op jit(solution)/shard_map/all_to_all | solution.py:139
  196.6 2.5 copy-start.9
  196.6 2.5 copy-start.11
  279.2 0.6 copy-start.10
Sparse Core Ops, SparseCore 0:
  10.1 56.0 all-gather.1
where the time goes:
time: 289 us; the launch traced here: 287 us
  other arithmetic  98.8 us (34%)
  loops' own time  53.6 us (19%)
  matrix products  38.8 us (13%)
  local copies, waits for them, and re-layouts  31.4 us (11%)
  waiting for transfers between devices  27.4 us (9%)
  starting transfers between devices  22.3 us (8%)
  between operations  14.3 us (5%)
    another operation x1, loops' own time, body(): lax.map(one_slot, (got_faces.reshape((slot_count,) + intersection_faces.s...  32.3 us
    reduce_sum x25, other arithmetic, correlate(): jnp.mean(magnitude, axis=(-2, -1), keepdims=True)  30.3 us
    convert_element_type x52, other arithmetic, dft_tables(): jnp.sin(angles).astype(jnp.bfloat16)  29.3 us
    another operation x1, loops' own time, body(): lax.map(coarse_one, (face_order // per_tile, partner_tiles, coarse_peaks))  21.4 us
    all_to_all x1, waiting for transfers between devices, body(): lax.all_to_all(parcel, 'tile', split_axis=0, concat_axis=0, tiled=True)  17.7 us
    dot_general x28, matrix products, spectrum(): jnp.einsum('...jky,jyl->...kl', segment_one, second_tables, preferred_ele...  13.9 us
    neg x26, other arithmetic, spectrum(): -sine_table  13.5 us
    dynamic_slice x16, local copies, waits for them, and re-layouts, body(): lax.map(coarse_one, (face_order // per_tile, partner_tiles, coarse_peaks))  10.2 us
  transfers between devices with their start and end apart: 6, of which 3 were waited for; matrix products, arithmetic and copies ran while one was open for 37% of the time, Pallas kernels for 0%

commit v1 on v0

--- a/solution.py
+++ b/solution.py
@@ -4,6 +4,29 @@
 from jax.sharding import PartitionSpec as P
 
 TWO_PI = 6.283185307179586
+
+
+def cut_along(shard, dim, size):
+    shape = shard.shape
+    pieces = shard.reshape(*shape[:dim], size, shape[dim] // size, *shape[dim + 1 :])
+    return jnp.moveaxis(pieces, dim, 0)
+
+
+def joined_along(blocks, dim):
+    shape = list(blocks.shape[1:])
+    shape[dim] *= blocks.shape[0]
+    return jnp.moveaxis(blocks, 0, dim).reshape(shape)
+
+
+def exchange_in_pairs(x, axis, split_dim, concat_dim):
+    size, index = (lax.axis_size(axis), lax.axis_index(axis))
+    parts = cut_along(x, split_dim, size)
+    gathered = [parts[index]]
+    for step in range(1, size):
+        sent = parts[index ^ step]
+        gathered.append(lax.ppermute(sent, axis, [(i, i ^ step) for i in range(size)]))
+    parts = jnp.stack(gathered)[index ^ jnp.arange(size)]
+    return joined_along(parts, concat_dim)
 
 
 def from_behind(value, axis, steps):
@@ -115,7 +138,7 @@
     parcel = parcel.reshape((tile_count, capacity) + intersection_faces.shape[1:])
     peak_marks = face_peaks[source].reshape((tile_count, capacity) + face_peaks.shape[1:])
     got_faces, got_marks, wanted_ids = (
-        lax.all_to_all(parcel, "tile", split_axis=0, concat_axis=0, tiled=True),
+        exchange_in_pairs(parcel, "tile", 0, 0),
         lax.all_to_all(peak_marks, "tile", split_axis=0, concat_axis=0, tiled=True),
         lax.all_to_all(requests, "tile", split_axis=0, concat_axis=0, tiled=True),
     )

time: 289 us -> 285 us (0.986)
  other arithmetic: 98.8 us -> 83.1 us
  local copies, waits for them, and re-layouts: 31.4 us -> 43.1 us
  waiting for transfers between devices: 27.4 us -> 20.7 us
  starting transfers between devices: 22.3 us -> 28.8 us
    all_to_all x1 -> x0, waiting for transfers between devices: 17.7 us -> none  [body(): lax.all_to_all(parcel, 'tile', split_axis=0, concat_axis=0, tiled=True)]
    ppermute x0 -> x7, waiting for transfers between devices: none -> 17.2 us  [exchange_in_pairs(): lax.ppermute(sent, axis, [(i, i ^ step) for i in range(size)])]
    reduce_sum x25, other arithmetic: 30.3 us -> 16.7 us  [correlate(): jnp.mean(magnitude, axis=(-2, -1), keepdims=True)]
    ppermute x0 -> x7, starting transfers between devices: none -> 10.6 us  [exchange_in_pairs(): lax.ppermute(sent, axis, [(i, i ^ step) for i in range(size)])]
    unnamed x24 -> x40, local copies, waits for them, and re-layouts: 0.96 us -> 7.28 us
    all_to_all x1 -> x0, starting transfers between devices: 3.49 us -> none  [body(): lax.all_to_all(parcel, 'tile', split_axis=0, concat_axis=0, tiled=True)]
    all_to_all x1, waiting for transfers between devices: 3.28 us -> 0.01 us  [body(): lax.all_to_all(peak_marks, 'tile', split_axis=0, concat_axis=0, tiled=True)]
    dynamic_slice x32 -> x64, local copies, waits for them, and re-layouts: 9.47 us -> 11.4 us  [body(): lax.map(one_slot, (got_faces.reshape((slot_count,) + intersection_faces.s...]
  transfers between devices with their start and end apart: 6 -> 12, of which waited for: 3 -> 4; matrix products, arithmetic and copies ran while one was open for 37% -> 37% of each run, Pallas kernels for 0% -> 0%
where the time goes in v1:
time: 285 us; the launch traced here: 284 us
  other arithmetic  83.1 us (29%)
  loops' own time  53.9 us (19%)
  local copies, waits for them, and re-layouts  43.1 us (15%)
  matrix products  39.8 us (14%)
  starting transfers between devices  28.8 us (10%)
  waiting for transfers between devices  20.7 us (7%)
  between operations  14.4 us (5%)
    another operation x1, loops' own time, body(): lax.map(one_slot, (got_faces.reshape((slot_count,) + intersection_faces.s...  32.5 us
    convert_element_type x52, other arithmetic, dft_tables(): jnp.sin(angles).astype(jnp.bfloat16)  29.9 us
    another operation x1, loops' own time, body(): lax.map(coarse_one, (face_order // per_tile, partner_tiles, coarse_peaks))  21.4 us
    ppermute x7, waiting for transfers between devices, exchange_in_pairs(): lax.ppermute(sent, axis, [(i, i ^ step) for i in range(size)])  17.2 us
    reduce_sum x25, other arithmetic, correlate(): jnp.mean(magnitude, axis=(-2, -1), keepdims=True)  16.7 us
    dot_general x28, matrix products, spectrum(): jnp.einsum('...jky,jyl->...kl', segment_one, second_tables, preferred_ele...  14.9 us
    neg x26, other arithmetic, spectrum(): -sine_table  13.6 us
    dynamic_slice x64, local copies, waits for them, and re-layouts, body(): lax.map(one_slot, (got_faces.reshape((slot_count,) + intersection_faces.s...  11.4 us
  transfers between devices with their start and end apart: 12, of which 4 were waited for; matrix products, arithmetic and copies ran while one was open for 37% of the time, Pallas kernels for 0%

profile of v1, /device:TPU:0, one launch (start us, length us, event | category | flops | bytes accessed | tf_op | source)
XLA Modules:
  0.0 283.8 jit_solution(8778719064940338810)
XLA Ops:
  9.7 1.3 gather_fusion
  11.7 7.3 %all-to-all-start = ((s32[8,1,2]{2,1,0:T(1,128)}), s32[8,1,2]{2,1,0:T(1,128)}, u32[]{:S(2)}, u32[]{:S(2)}) async-start(s32[8,1,2]{2,1,0:T(1,128)} %bitcast.34), calls=%async_computation | async-start | bytes 8192 | tf_op jit(solution)/shard_map/all_to_all | solution.py:143
  19.0 2.1 collective-permute-start.7
  21.2 1.7 gather_fusion.2
  23.9 4.6 %collective-permute-start.6 = (bf16[1,2,1,128,128]{4,3,1,2,0:T(8,128)(2,1)}, bf16[1,2,1,128,128]{4,3,1,2,0:T(8,128)(2,1)}, u32[]{:S(2)}, u32[]{:S(2)}) collective-permute-start(bf16[1,2,1,128,128]{4,3,1,2,0:T(8,128)(2,1)} %get-tuple-element.293), channel_id=1, source_target_pairs={{0,7},{1,6},{2,5},{3,4},{4,3},{5,2},{6,1},{7,0},{8,15},{9,14},{10,... | collective-permute-start | bytes 196616 | tf_op jit(solution)/shard_map/ppermute | solution.py:27
  29.5 1.5 collective-permute-start
  33.0 1.0 fusion.217
  34.0 1.7 sine_convert_fusion.5
  35.7 1.1 sine_convert_fusion.4
  40.5 1.9 convolution_bitcast_fusion.2
  43.0 1.3 gather_fusion.1
  44.3 4.5 %all-to-all-start.1 = ((s32[8,2,2,8]{3,2,1,0:T(2,128)}), s32[8,2,2,8]{3,2,1,0:T(2,128)S(1)}, u32[]{:S(2)}, u32[]{:S(2)}) async-start(s32[8,2,2,8]{3,2,1,0:T(2,128)} %bitcast.35), calls=%async_computation.1 | async-start | bytes 32768 | tf_op jit(solution)/shard_map/all_to_all | solution.py:142
  49.4 1.3 reduce.15
  50.8 2.1 collective-permute-start.1
  52.9 1.5 bitcast_dynamic-update-slice_fusion.6
  54.4 4.9 %collective-permute-done.1 = bf16[1,2,1,128,128]{4,3,1,2,0:T(8,128)(2,1)S(1)} collective-permute-done((bf16[1,2,1,128,128]{4,3,1,2,0:T(8,128)(2,1)}, bf16[1,2,1,128,128]{4,3,1,2,0:T(8,128)(2,1)S(1)}, u32[]{:S(2)}, u32[]{:S(2)}) %collective-permute-start.1) | collective-permute-done | bytes 65568 | tf_op jit(solution)/shard_map/ppermute | solution.py:27
  60.6 7.6 %collective-permute-done.2 = bf16[1,2,1,128,128]{4,3,1,2,0:T(8,128)(2,1)S(1)} collective-permute-done((bf16[1,2,1,128,128]{4,3,1,2,0:T(8,128)(2,1)}, bf16[1,2,1,128,128]{4,3,1,2,0:T(8,128)(2,1)S(1)}, u32[]{:S(2)}, u32[]{:S(2)}) %collective-permute-start.2) | collective-permute-done | bytes 65568 | tf_op jit(solution)/shard_map/ppermute | solution.py:27
  69.5 4.6 %collective-permute-done.3 = bf16[1,2,1,128,128]{4,3,1,2,0:T(8,128)(2,1)S(1)} collective-permute-done((bf16[1,2,1,128,128]{4,3,1,2,0:T(8,128)(2,1)}, bf16[1,2,1,128,128]{4,3,1,2,0:T(8,128)(2,1)S(1)}, u32[]{:S(2)}, u32[]{:S(2)}) %collective-permute-start.3) | collective-permute-done | bytes 65568 | tf_op jit(solution)/shard_map/ppermute | solution.py:27
  74.8 1.5 bitcast_dynamic-update-slice_fusion.2
  76.3 1.5 bitcast_dynamic-update-slice_fusion.1
  77.7 1.5 bitcast_dynamic-update-slice_fusion
  79.2 1.7 gather_fusion.3
  80.9 100.8 %while.24 = (s32[]{:T(128)}, f32[16,1,8]{2,1,0:T(1,128)}, s32[16]{0:T(128)S(1)}, s32[16,2,8]{2,1,0:T(2,128)S(1)}, bf16[16,1,128,128]{3,2,0,1:T(8,128)(2,1)S(1)},...) while((s32[]{:T(128)}, f32[16,1,8]{2,1,0:T(1,128)}, ...), condition=%wide.region_6.7_spmd, body=%wide.region_3.6_spmd.sunk | while | flops 33161740 | bytes 1854074 | solution.py:154
  181.7 4.2 %all-to-all-start.2 = ((f32[8,2,1,8]{3,1,2,0:T(2,128)}), f32[8,2,1,8]{3,1,2,0:T(2,128)S(1)}, u32[]{:S(2)}, u32[]{:S(2)}) async-start(f32[8,2,1,8]{3,1,2,0:T(2,128)} %bitcast.371), calls=%async_computation.2 | async-start | bytes 16384 | tf_op jit(solution)/shard_map/all_to_all | solution.py:162
  186.0 1.3 convolution_bitcast_fusion.4
  189.6 2.9 %all-to-all-done.2 = f32[8,2,1,8]{3,1,2,0:T(2,128)S(1)} async-done(((f32[8,2,1,8]{3,1,2,0:T(2,128)}), f32[8,2,1,8]{3,1,2,0:T(2,128)S(1)}, u32[]{:S(2)}, u32[]{:S(2)}) %all-to-all-start.2) | async-done | bytes 544 | tf_op jit(solution)/shard_map/all_to_all | solution.py:162
  192.4 1.3 gather_fusion.4
  193.7 2.3 gather_fusion.5
  196.2 80.1 %while.25 = (s32[]{:T(128)}, f32[8,8]{1,0:T(8,128)S(1)}, s32[8,2,8]{2,1,0:T(2,128)}, s32[8]{0:T(128)S(1)}, f32[2,256,256]{2,1,0:T(8,128)S(1)}, /*index=5*/bf16[8...) while((s32[]{:T(128)}, f32[8,8]{1,0:T(8,128)S(1)}, ...), condition=%wide.region_10.11_spmd, body=%wide.region_7.10_spmd.sunk | while | flops 232903680 | bytes 6737723 | solution.py:185
  199.5 1.0 fusion.345
  200.5 1.1 sine_convert_fusion.15
  201.6 1.1 sine_convert_fusion.14
  209.5 1.0 fusion.345
  210.5 1.1 sine_convert_fusion.15
  211.6 1.1 sine_convert_fusion.14
  219.5 1.0 fusion.345
  220.5 1.1 sine_convert_fusion.15
  221.6 1.1 sine_convert_fusion.14
  230.5 1.1 sine_convert_fusion.15
  231.7 1.1 sine_convert_fusion.14
  240.6 1.1 sine_convert_fusion.15
  241.7 1.1 sine_convert_fusion.14
  250.6 1.1 sine_convert_fusion.15
  251.7 1.1 sine_convert_fusion.14
  260.6 1.1 sine_convert_fusion.15
  261.7 1.1 sine_convert_fusion.14
  270.6 1.1 sine_convert_fusion.15
  271.7 1.1 sine_convert_fusion.14
  (515 shorter events, 124.9 us)
Async XLA Ops:
  7.2 35.8 %copy-start = (s32[8,2,8]{2,1,0:T(2,128)S(1)}, s32[8,2,8]{2,1,0:T(2,128)}, u32[]{:S(2)}) copy-start(s32[8,2,8]{2,1,0:T(2,128)} %param.16) | copy-start | bytes 1540
  7.2 24.4 %copy-start.13 = (s32[8,1]{0,1:T(1,128)S(1)}, s32[8,1]{0,1:T(1,128)}, u32[]{:S(2)}) copy-start(s32[8,1]{0,1:T(1,128)} %param.14) | copy-start | bytes 100
  7.2 24.4 %copy-start.1 = (s32[8]{0:T(128)S(1)}, s32[8]{0:T(128)}, u32[]{:S(2)}) copy-start(s32[8]{0:T(128)} %param.15) | copy-start | bytes 100
  7.2 186.5 %all-gather.2.cloned.1.call-start = ((), (), s32[]{:S(2)}) async-start(), calls=%async_computation.3 | async-start | bytes 2359296 | tf_op jit(solution)/shard_map/all_gather | solution.py:173
  9.7 22.7 %copy-start.9 = (s32[1024]{0:T(1024)}, s32[1024]{0:T(1024)S(1)}, u32[]{:S(2)}) copy-start(s32[1024]{0:T(1024)S(1)} %pad_clamp_fusion.3) | copy-start | bytes 12292
  11.0 26.4 %copy-start.11 = (s32[2,2,8]{2,1,0:T(2,128)S(1)}, s32[2,2,8]{2,1,0:T(2,128)}, u32[]{:S(2)}) copy-start(s32[2,2,8]{2,1,0:T(2,128)} %param.21) | copy-start | bytes 388
  11.7 32.6 %all-to-all-start = ((s32[8,1,2]{2,1,0:T(1,128)}), s32[8,1,2]{2,1,0:T(1,128)}, u32[]{:S(2)}, u32[]{:S(2)}) async-start(s32[8,1,2]{2,1,0:T(1,128)} %bitcast.34), calls=%async_computation | async-start | bytes 8192 | tf_op jit(solution)/shard_map/all_to_all | solution.py:143
  19.0 166.9 %collective-permute-start.7 = (bf16[2,1,128,128]{3,2,1,0:T(8,128)(2,1)}, bf16[2,1,128,128]{3,2,1,0:T(8,128)(2,1)}, u32[]{:S(2)}, u32[]{:S(2)}) collective-permute-start(bf16[2,1,128,128]{3,2,1,0:T(8,128)(2,1)} %param.20), channel_id=1, source_target_pairs={{0,8},{8,16},{16,24},{1,9},{9,17},{17,25},{2,10},{10,18},{18,26},{... | collective-permute-start | bytes 196616 | tf_op jit(solution)/shard_map/ppermute | solution.py:35
  21.2 18.1 %copy-start.2 = (bf16[8,1,128,128]{3,2,1,0:T(8,128)(2,1)S(1)}, bf16[8,1,128,128]{3,2,1,0:T(8,128)(2,1)}, u32[]{:S(2)}) copy-start(bf16[8,1,128,128]{3,2,1,0:T(8,128)(2,1)} %param.13) | copy-start | bytes 786436
  22.9 17.1 %copy-start.7 = (bf16[2,1,128,128]{3,2,1,0:T(8,128)(2,1)S(1)}, bf16[2,1,128,128]{3,2,1,0:T(8,128)(2,1)}, u32[]{:S(2)}) copy-start(bf16[2,1,128,128]{3,2,1,0:T(8,128)(2,1)} %param.19) | copy-start | bytes 196612
  23.9 53.9 %collective-permute-start.6 = (bf16[1,2,1,128,128]{4,3,1,2,0:T(8,128)(2,1)}, bf16[1,2,1,128,128]{4,3,1,2,0:T(8,128)(2,1)}, u32[]{:S(2)}, u32[]{:S(2)}) collective-permute-start(bf16[1,2,1,128,128]{4,3,1,2,0:T(8,128)(2,1)} %get-tuple-element.293), channel_id=1, source_target_pairs={{0,7},{1,6},{2,5},{3,4},{4,3},{5,2},{6,1},{7,0},{8,15},{9,14},{10,... | collective-permute-start | bytes 196616 | tf_op jit(solution)/shard_map/ppermute | solution.py:27
  28.4 47.9 %collective-permute-start.5 = (bf16[1,2,1,128,128]{4,3,1,2,0:T(8,128)(2,1)}, bf16[1,2,1,128,128]{4,3,1,2,0:T(8,128)(2,1)}, u32[]{:S(2)}, u32[]{:S(2)}) collective-permute-start(bf16[1,2,1,128,128]{4,3,1,2,0:T(8,128)(2,1)} %get-tuple-element.294), channel_id=1, source_target_pairs={{0,6},{1,7},{2,4},{3,5},{4,2},{5,3},{6,0},{7,1},{8,14},{9,15},{10,... | collective-permute-start | bytes 196616 | tf_op jit(solution)/shard_map/ppermute | solution.py:27
  29.0 45.8 %collective-permute-start.4 = (bf16[1,2,1,128,128]{4,3,1,2,0:T(8,128)(2,1)}, bf16[1,2,1,128,128]{4,3,1,2,0:T(8,128)(2,1)}, u32[]{:S(2)}, u32[]{:S(2)}) collective-permute-start(bf16[1,2,1,128,128]{4,3,1,2,0:T(8,128)(2,1)} %get-tuple-element.295), channel_id=1, source_target_pairs={{0,5},{1,4},{2,7},{3,6},{4,1},{5,0},{6,3},{7,2},{8,13},{9,12},{10,... | collective-permute-start | bytes 196616 | tf_op jit(solution)/shard_map/ppermute | solution.py:27
  29.5 21.3 %collective-permute-start = (bf16[1,2,1,128,128]{4,3,1,2,0:T(8,128)(2,1)}, bf16[1,2,1,128,128]{4,3,1,2,0:T(8,128)(2,1)}, u32[]{:S(2)}, u32[]{:S(2)}) collective-permute-start(bf16[1,2,1,128,128]{4,3,1,2,0:T(8,128)(2,1)} %get-tuple-element.299), channel_id=1, source_target_pairs={{0,1},{1,0},{2,3},{3,2},{4,5},{5,4},{6,7},{7,6},{8,9},{9,8},{10,11... | collective-permute-start | bytes 196616 | tf_op jit(solution)/shard_map/ppermute | solution.py:27
  32.7 7.8 %copy-start.3 = (bf16[1,128,128]{2,1,0:T(8,128)(2,1)}, bf16[1,128,128]{2,1,0:T(8,128)(2,1)S(1)}, u32[]{:S(2)}) copy-start(bf16[1,128,128]{2,1,0:T(8,128)(2,1)S(1)} %get-tuple-element.313) | copy-start | bytes 98308
  32.7 7.8 %copy-start.5 = (bf16[1,128,128]{2,1,0:T(8,128)(2,1)}, bf16[1,128,128]{2,1,0:T(8,128)(2,1)S(1)}, u32[]{:S(2)}) copy-start(bf16[1,128,128]{2,1,0:T(8,128)(2,1)S(1)} %get-tuple-element.314) | copy-start | bytes 98308
  42.4 0.6 copy-start.12
  44.3 36.6 %all-to-all-start.1 = ((s32[8,2,2,8]{3,2,1,0:T(2,128)}), s32[8,2,2,8]{3,2,1,0:T(2,128)S(1)}, u32[]{:S(2)}, u32[]{:S(2)}) async-start(s32[8,2,2,8]{3,2,1,0:T(2,128)} %bitcast.35), calls=%async_computation.1 | async-start | bytes 32768 | tf_op jit(solution)/shard_map/all_to_all | solution.py:142
  50.8 8.4 %collective-permute-start.1 = (bf16[1,2,1,128,128]{4,3,1,2,0:T(8,128)(2,1)}, bf16[1,2,1,128,128]{4,3,1,2,0:T(8,128)(2,1)S(1)}, u32[]{:S(2)}, u32[]{:S(2)}) collective-permute-start(bf16[1,2,1,128,128]{4,3,1,2,0:T(8,128)(2,1)} %get-tuple-element.298), channel_id=1, source_target_pairs={{0,2},{1,3},{2,0},{3,1},{4,6},{5,7},{6,4},{7,5},{8,10},{9,11},{10,... | collective-permute-start | bytes 196616 | tf_op jit(solution)/shard_map/ppermute | solution.py:27
  59.2 9.0 %collective-permute-start.2 = (bf16[1,2,1,128,128]{4,3,1,2,0:T(8,128)(2,1)}, bf16[1,2,1,128,128]{4,3,1,2,0:T(8,128)(2,1)S(1)}, u32[]{:S(2)}, u32[]{:S(2)}) collective-permute-start(bf16[1,2,1,128,128]{4,3,1,2,0:T(8,128)(2,1)} %get-tuple-element.297), channel_id=1, source_target_pairs={{0,3},{1,2},{2,1},{3,0},{4,7},{5,6},{6,5},{7,4},{8,11},{9,10},{10,... | collective-permute-start | bytes 196616 | tf_op jit(solution)/shard_map/ppermute | solution.py:27
  68.3 5.9 %collective-permute-start.3 = (bf16[1,2,1,128,128]{4,3,1,2,0:T(8,128)(2,1)}, bf16[1,2,1,128,128]{4,3,1,2,0:T(8,128)(2,1)S(1)}, u32[]{:S(2)}, u32[]{:S(2)}) collective-permute-start(bf16[1,2,1,128,128]{4,3,1,2,0:T(8,128)(2,1)} %get-tuple-element.296), channel_id=1, source_target_pairs={{0,4},{1,5},{2,6},{3,7},{4,0},{5,1},{6,2},{7,3},{8,12},{9,13},{10,... | collective-permute-start | bytes 196616 | tf_op jit(solution)/shard_map/ppermute | solution.py:27
  80.9 105.0 %copy-start.4 = (bf16[1,128,128]{2,1,0:T(8,128)(2,1)S(1)}, bf16[1,128,128]{2,1,0:T(8,128)(2,1)}, u32[]{:S(2)}) copy-start(bf16[1,128,128]{2,1,0:T(8,128)(2,1)} %copy-done.3) | copy-start | bytes 98308
  80.9 105.0 %copy-start.6 = (bf16[1,128,128]{2,1,0:T(8,128)(2,1)S(1)}, bf16[1,128,128]{2,1,0:T(8,128)(2,1)}, u32[]{:S(2)}) copy-start(bf16[1,128,128]{2,1,0:T(8,128)(2,1)} %copy-done.5) | copy-start | bytes 98308
  181.7 6.6 %copy-start.8 = (s32[2,1,1,8]{3,2,0,1:T(1,128)S(1)}, s32[2,1,1,8]{3,2,0,1:T(1,128)}, u32[]{:S(2)}) copy-start(s32[2,1,1,8]{3,2,0,1:T(1,128)} %get-tuple-element.307) | copy-start | bytes 196
  181.7 10.7 %all-to-all-start.2 = ((f32[8,2,1,8]{3,1,2,0:T(2,128)}), f32[8,2,1,8]{3,1,2,0:T(2,128)S(1)}, u32[]{:S(2)}, u32[]{:S(2)}) async-start(f32[8,2,1,8]{3,1,2,0:T(2,128)} %bitcast.371), calls=%async_computation.2 | async-start | bytes 16384 | tf_op jit(solution)/shard_map/all_to_all | solution.py:162
  187.3 8.8 %copy-start.10 = (pred[8]{0:T(512)(128)(4,1)S(1)}, pred[8]{0:T(512)(128)(4,1)}, u32[]{:S(2)}) copy-start(pred[8]{0:T(512)(128)(4,1)} %get-tuple-element.265) | copy-start | bytes 28
  193.7 2.5 copy-start.14
  193.7 2.5 copy-start.16
  276.3 0.6 copy-start.15
Sparse Core Ops, SparseCore 0:
  10.2 59.1 all-gather.1
